TPU v7x, 32 devices: a whole 2x2x4 slice. The times are simulated.
32 devices in a mesh: ens: 2 (over y), patch: 4 (over z), mp: 4 (over x, core).
Axes of the slice: x: 2, y: 2, z: 4, core: 2. Of those that a mesh axis runs over, the one named last changes fastest.
Arguments:
- grid_in: bfloat16 [84, 4096], P(None, ('ens', 'patch')), parts along dimension 1, may hold values from -6 to 6
- mesh_static: bfloat16 [1024, 512], P('patch'), may hold values from -50 to 50
- embed_weight: bfloat16 [84, 512], replicated, may hold values from -0.625 to 0.625
- embed_bias: float32 [512], replicated, may hold values from -3 to 3
- encode_source: bfloat16 [512, 512], P(None, 'mp'), may hold values from -0.25 to 0.25
- encode_target: bfloat16 [512, 512], P(None, 'mp'), may hold values from -0.25 to 0.25
- encode_edge: bfloat16 [4, 512], P(None, 'mp'), may hold values from -3 to 3
- encode_bias: float32 [512], P('mp'), may hold values from -3 to 3
- encode_out: bfloat16 [512, 512], P('mp'), may hold values from -0.125 to 0.125
- layer_gain: float32 [2, 512], replicated, may hold values from 0.5 to 1.5
- attention_in: bfloat16 [2, 512, 3, 512], P(None, None, None, 'mp'), may hold values from -0.25 to 0.25
- query_gain: float32 [2, 128], replicated, may hold values from 0.5 to 2.5
- key_gain: float32 [2, 128], replicated, may hold values from 0.5 to 2.5
- attention_out: bfloat16 [2, 512, 512], P(None, 'mp'), may hold values from -0.25 to 0.25
- hidden_in: bfloat16 [2, 512, 2048], P(None, None, 'mp'), may hold values from -0.25 to 0.25
- hidden_out: bfloat16 [2, 2048, 512], P(None, 'mp'), may hold values from -0.125 to 0.125
- final_gain: float32 [512], replicated, may hold values from 0.5 to 1.5
- decode_node: bfloat16 [512, 512], P(None, 'mp'), may hold values from -0.25 to 0.25
- decode_grid: bfloat16 [512, 512], P(None, 'mp'), may hold values from -0.25 to 0.25
- decode_bias: float32 [512], P('mp'), may hold values from -3 to 3
- decode_out: bfloat16 [512, 84], P('mp'), may hold values from -0.25 to 0.25
- cell_lists: int32 [4, 4, 256], P('patch'), may hold values from 0 to 511
- edge_source: int32 [4, 1024], P('patch'), may hold values from 0 to 1535, as said below
- edge_target: int32 [4, 1024], P('patch'), may hold values from 0 to 256, as said below
- edge_geometry: bfloat16 [4, 4, 1024], P('patch'), may hold values from -6 to 6
- halo_lists: int32 [4, 4, 128], P('patch'), may hold values from 0 to 255
- neighbours: int32 [4, 32, 256], P('patch'), may hold values from 0 to 767, as said below
- node_lists: int32 [4, 4, 128], P('patch'), may hold values from 0 to 255
- cell_nodes: int32 [3, 2048], P(None, 'patch'), may hold values from 0 to 767, as said below
Outputs:
- denoised: bfloat16 [84, 4096], P(None, ('ens', 'patch')), parts along dimension 1
There are 2 independent parts, one for each index of `ens`. A program takes and returns all parts, laid end to end along the dimension named above; an argument that names none is the same for every part. Nothing has to cross between parts.
Inputs may be any that keep to these rules, and one draw needn't show every extreme that they name: `cell_lists`: entry [p, k, j] is a cell of band p, numbered within the band, sent as row j of band p's list for patch p + b_k; entries may repeat. `edge_source`: entry [p, e] is the sender row of edge slot e of patch p in cell_table_p: below 512 a cell of band p, else row 512 + k * 256 + j, entry j of the list that band p - b_k sends; never a list of a band beyond the ends. `edge_target`: entry [p, e] is the receiving node of edge slot e of patch p, numbered within the patch; 256 marks padding, which stands only after all real edges of the patch; real receivers ascend along a patch's row; the first and the last patch have no padding. `halo_lists`: entry [p, k, j] is a node of patch p sent as row j of its key list for patch p + b_k; entries may repeat. `neighbours`: entry [p, n, i] is the n-th key of node i of patch p in key_table_p: below 256 a node of patch p, else row 256 + k * 128 + j, entry j of the key list that patch p - b_k sends; never a list of a patch beyond the ends; keys may repeat. `node_lists`: entry [p, k, j] is a node of patch p sent as row j of its decoder list for band p + b_k; entries may repeat. `cell_nodes`: entry [j, g] is a row of node_table_p for the band p of cell g: below 256 a node of patch p, else row 256 + k * 128 + i, entry i of the decoder list that patch p - b_k sends; never a list of a patch beyond the ends.
All inputs are finite; a program needn't handle non-finite values.
Results may differ from a plain program's by a relative error of at most 0.02.
Values may be sent and summed in bfloat16 or wider, within the bound.
A program may use at most 64 MiB of HBM per device.

v0:
```python
import math

import jax
import jax.numpy as jnp
from jax import lax
from jax.sharding import PartitionSpec as P

LAYERS = 2


norm_epsilon = 1e-05


def passed_along(value, axis, steps):
    count = lax.axis_size(axis)
    initial, last = (max(0, -steps), min(count, count - steps))
    return lax.ppermute(value, axis, [(source, source + steps) for source in range(initial, last)])


def offset_of(number):
    return (number // 2 + 1) * (1 if number % 2 == 0 else -1)


def layer_norm(values, norm_gain):
    average = jnp.mean(values, axis=-1, keepdims=True)
    centred = values - average
    spread = jnp.mean(centred * centred, axis=-1, keepdims=True)
    return centred * lax.rsqrt(spread + norm_epsilon) * norm_gain


def rms_scale(values, norm_gain):
    return (
        values
        * lax.rsqrt(jnp.mean(values * values, axis=-1, keepdims=True) + norm_epsilon)
        * norm_gain
    )


def one_hot_rows(targets, node_count):
    row_ids = lax.broadcasted_iota(jnp.int32, (node_count, targets.shape[0]), 0)
    return (row_ids == targets[None, :]).astype(jnp.bfloat16)


def width_total(partial_term):
    return lax.psum(partial_term.astype(jnp.bfloat16), "mp").astype(jnp.float32)


def send_cells(sections):
    return [
        passed_along(section, "patch", offset_of(number)) for number, section in enumerate(sections)
    ]


def send_nodes(sections):
    return [
        passed_along(section, "patch", offset_of(number)) for number, section in enumerate(sections)
    ]


def send_halo(outgoing):
    near_count = outgoing.shape[0]
    return jnp.stack(
        [passed_along(outgoing[number], "patch", offset_of(number)) for number in range(near_count)]
    )


def shards(
    grid_in,
    mesh_static,
    embed_weight,
    embed_bias,
    encode_source,
    encode_target,
    encode_edge,
    encode_bias,
    encode_out,
    layer_gain,
    attention_in,
    query_gain,
    key_gain,
    attention_out,
    hidden_in,
    hidden_out,
    final_gain,
    decode_node,
    decode_grid,
    decode_bias,
    decode_out,
    cell_lists,
    edge_source,
    edge_target,
    edge_geometry,
    halo_lists,
    neighbours,
    node_lists,
    cell_nodes,
):
    channel_dims = (((0,), (0,)), ((), ()))
    grid_latent = jax.nn.silu(
        lax.dot_general(grid_in, embed_weight, channel_dims, preferred_element_type=jnp.float32)
        + embed_bias
    ).astype(jnp.bfloat16)
    node_count = mesh_static.shape[0]
    near_count = cell_lists.shape[1]
    projected = jnp.dot(grid_latent, encode_source, preferred_element_type=jnp.float32).astype(
        jnp.bfloat16
    )
    outgoing_cells = jnp.take(projected, cell_lists[0], axis=0)
    arrived = jnp.concatenate(
        send_cells([outgoing_cells[number] for number in range(near_count)]), axis=0
    )
    cell_table = jnp.concatenate([projected, arrived], axis=0)
    target_part = jnp.dot(mesh_static, encode_target, preferred_element_type=jnp.float32).astype(
        jnp.bfloat16
    )
    targets = edge_target[0]
    source_rows = jnp.take(cell_table, edge_source[0], axis=0)
    target_rows = jnp.take(target_part, jnp.minimum(targets, node_count - 1), axis=0)
    geometry_term = lax.dot_general(
        edge_geometry[0], encode_edge, channel_dims, preferred_element_type=jnp.float32
    )
    messages = jax.nn.silu(
        source_rows.astype(jnp.float32)
        + target_rows.astype(jnp.float32)
        + geometry_term
        + encode_bias
    ).astype(jnp.bfloat16)
    gathered = jnp.dot(
        one_hot_rows(targets, node_count), messages, preferred_element_type=jnp.float32
    ).astype(jnp.bfloat16)
    latent = mesh_static.astype(jnp.float32) + width_total(
        jnp.dot(gathered, encode_out, preferred_element_type=jnp.float32)
    )
    head_width = query_gain.shape[1]
    for layer_index in range(LAYERS):
        normed = layer_norm(latent, layer_gain[layer_index]).astype(jnp.bfloat16)
        projections = lax.dot_general(
            normed,
            attention_in[layer_index],
            (((1,), (0,)), ((), ())),
            preferred_element_type=jnp.float32,
        )
        local_width = projections.shape[2]
        query_matrix = rms_scale(
            projections[:, 0].reshape(node_count, -1, head_width), query_gain[layer_index]
        ).astype(jnp.bfloat16)
        key_rows = rms_scale(
            projections[:, 1].reshape(node_count, -1, head_width), key_gain[layer_index]
        ).astype(jnp.bfloat16)
        key_value = jnp.concatenate(
            [key_rows.reshape(node_count, local_width), projections[:, 2].astype(jnp.bfloat16)],
            axis=1,
        )
        outgoing_halo = jnp.take(key_value, halo_lists[0], axis=0)
        halo_table = jnp.concatenate(
            [key_value, send_halo(outgoing_halo).reshape(-1, 2 * local_width)], axis=0
        )
        selected_entries = jnp.take(halo_table, neighbours[0], axis=0)
        key_count = selected_entries.shape[0]
        selected_keys = selected_entries[:, :, :local_width].reshape(
            key_count, node_count, -1, head_width
        )
        selected_values = selected_entries[:, :, local_width:].reshape(
            key_count, node_count, -1, head_width
        )
        attention_logits = jnp.einsum(
            "ave,gave->avg", query_matrix, selected_keys, preferred_element_type=jnp.float32
        ) / math.sqrt(head_width)
        weights = jnp.exp(attention_logits)
        softmax_weights = (weights / jnp.sum(weights, axis=-1, keepdims=True)).astype(jnp.bfloat16)
        attended = (
            jnp.einsum(
                "rby,yrbg->rbg",
                softmax_weights,
                selected_values,
                preferred_element_type=jnp.float32,
            )
            .astype(jnp.bfloat16)
            .reshape(node_count, local_width)
        )
        hidden = jax.nn.silu(
            jnp.dot(normed, hidden_in[layer_index], preferred_element_type=jnp.float32)
        ).astype(jnp.bfloat16)
        partial_term = jnp.dot(
            attended, attention_out[layer_index], preferred_element_type=jnp.float32
        ) + jnp.dot(hidden, hidden_out[layer_index], preferred_element_type=jnp.float32)
        latent = latent + width_total(partial_term)
    final_normed = layer_norm(latent, final_gain).astype(jnp.bfloat16)
    node_part = jnp.dot(final_normed, decode_node, preferred_element_type=jnp.float32).astype(
        jnp.bfloat16
    )
    outgoing_nodes = jnp.take(node_part, node_lists[0], axis=0)
    node_table = jnp.concatenate(
        [node_part] + send_nodes([outgoing_nodes[number] for number in range(near_count)]), axis=0
    )
    grid_part = jnp.dot(grid_latent, decode_grid, preferred_element_type=jnp.float32) + decode_bias
    chosen_nodes = jnp.take(node_table, cell_nodes, axis=0)
    activity = jnp.sum(
        jax.nn.silu(chosen_nodes.astype(jnp.float32) + grid_part[None]), axis=0
    ).astype(jnp.bfloat16)
    output_term = lax.dot_general(
        decode_out, activity, (((0,), (1,)), ((), ())), preferred_element_type=jnp.float32
    )
    return lax.psum(output_term.astype(jnp.bfloat16), "mp")


def solution(mesh):
    in_specs = (
        P(None, ("ens", "patch")),
        P("patch", None),
        P(),
        P(),
        P(None, "mp"),
        P(None, "mp"),
        P(None, "mp"),
        P("mp"),
        P("mp", None),
        P(),
        P(None, None, None, "mp"),
        P(),
        P(),
        P(None, "mp", None),
        P(None, None, "mp"),
        P(None, "mp", None),
        P(),
        P(None, "mp"),
        P(None, "mp"),
        P("mp"),
        P("mp", None),
        P("patch", None, None),
        P("patch", None),
        P("patch", None),
        P("patch", None, None),
        P("patch", None, None),
        P("patch", None, None),
        P("patch", None, None),
        P(None, "patch"),
    )
    out_specs = P(None, ("ens", "patch"))
    return jax.shard_map(shards, mesh=mesh, in_specs=in_specs, out_specs=out_specs, check_vma=False)
```

profile of v0, /device:TPU:0, one launch (start us, length us, event | category | flops | bytes accessed | tf_op | source)
XLA Modules:
  0.0 338.4 jit_solution(5244364710956704604)
XLA Ops:
  8.7 1.5 multiply_convert_fusion
  11.1 3.2 gather_fusion
  15.2 5.5 %collective-permute-start = (bf16[256,128]{1,0:T(8,128)(2,1)}, bf16[256,128]{1,0:T(8,128)(2,1)}, u32[]{:S(2)}, u32[]{:S(2)}) collective-permute-start(bf16[256,128]{1,0:T(8,128)(2,1)} %get-tuple-element.30), channel_id=1, source_target_pairs={{0,4},{4,8},{8,12},{1,5},{5,9},{9,13},{2,6},{6,10},{10,14},{3,7},{... | collective-permute-start | bytes 196616 | tf_op jit(solution)/shard_map/ppermute | solution.py:17
  22.1 5.6 %collective-permute-start.2 = (bf16[256,128]{1,0:T(8,128)(2,1)}, bf16[256,128]{1,0:T(8,128)(2,1)}, u32[]{:S(2)}, u32[]{:S(2)}) collective-permute-start(bf16[256,128]{1,0:T(8,128)(2,1)} %get-tuple-element.28), channel_id=1, source_target_pairs={{0,8},{4,12},{1,9},{5,13},{2,10},{6,14},{3,11},{7,15},{16,24},{20,... | collective-permute-start | bytes 196616 | tf_op jit(solution)/shard_map/ppermute | solution.py:17
  35.8 3.2 gather_fusion.2
  42.5 3.2 gather_fusion.1
  45.8 2.4 convolution_convert_fusion
  48.3 35.4 %all-reduce.5.cloned.1.call-done = bf16[256,512]{1,0:T(8,128)(2,1)} async-done(((bf16[256,512]{1,0:T(8,128)(2,1)}), bf16[256,512]{1,0:T(8,128)(2,1)}) %all-reduce.5.cloned.1.call-update) | async-done | bytes 262160 | tf_op jit(solution)/shard_map/psum | solution.py:45
  87.7 2.0 gather_fusion.5
  89.8 3.4 %collective-permute-start.4 = (bf16[128,256]{1,0:T(8,128)(2,1)S(1)}, bf16[128,256]{1,0:T(8,128)(2,1)S(1)}, u32[]{:S(2)}, u32[]{:S(2)}) collective-permute-start(bf16[128,256]{1,0:T(8,128)(2,1)S(1)} %get-tuple-element.23), channel_id=1, source_target_pairs={{0,4},{4,8},{8,12},{1,5},{5,9},{9,13},{2,6},{6,10},{10,14},{3,7},{... | collective-permute-start | bytes 196616 | tf_op jit(solution)/shard_map/ppermute | solution.py:17
  94.5 5.5 %collective-permute-start.6 = (bf16[128,256]{1,0:T(8,128)(2,1)S(1)}, bf16[128,256]{1,0:T(8,128)(2,1)S(1)}, u32[]{:S(2)}, u32[]{:S(2)}) collective-permute-start(bf16[128,256]{1,0:T(8,128)(2,1)S(1)} %get-tuple-element.25), channel_id=1, source_target_pairs={{0,8},{4,12},{1,9},{5,13},{2,10},{6,14},{3,11},{7,15},{16,24},{20,... | collective-permute-start | bytes 196616 | tf_op jit(solution)/shard_map/ppermute | solution.py:17
  101.3 2.5 fusion.11
  104.6 2.5 collective-permute-done.7
  107.2 32.9 %gather_fusion.6 = bf16[8192,256]{1,0:T(8,128)(2,1)} fusion(bf16[768,256]{1,0:T(8,128)(2,1)S(1)} %pad_maximum_fusion, s32[8192]{0:T(1024)S(1)} %broadcast_clamp_fusion), kind=kCustom, calls=%fused_computation.1.clone | custom fusion | bytes 8421376 | tf_op jit(solution)/shard_map/jit(_take)/gather | solution.py:158
  140.1 3.6 %broadcast_select_fusion.1 = bf16[32,256,256]{2,1,0:T(8,128)(2,1)S(1)} fusion(bf16[32,256,256]{2,1,0:T(8,128)(2,1)} %bitcast.192, pred[32,256]{1,0:T(8,128)(4,1)S(1)} %compare_and_fusion), kind=kLoop, calls=%fused_computation.12 | loop fusion | flops 2097152 | bytes 8396800 | tf_op jit(solution)/shard_map/jit(_take)/select_n | solution.py:158
  147.3 2.0 fusion.4
  150.1 30.0 %all-reduce.7.cloned.1.call-done = bf16[256,512]{1,0:T(8,128)(2,1)} async-done(((bf16[256,512]{1,0:T(8,128)(2,1)}), bf16[256,512]{1,0:T(8,128)(2,1)}) %all-reduce.7.cloned.1.call-update) | async-done | bytes 262160 | tf_op jit(solution)/shard_map/psum | solution.py:45
  183.8 2.0 gather_fusion.7
  185.9 3.4 %collective-permute-start.8 = (bf16[128,256]{1,0:T(8,128)(2,1)S(1)}, bf16[128,256]{1,0:T(8,128)(2,1)S(1)}, u32[]{:S(2)}, u32[]{:S(2)}) collective-permute-start(bf16[128,256]{1,0:T(8,128)(2,1)S(1)} %get-tuple-element.19), channel_id=1, source_target_pairs={{0,4},{4,8},{8,12},{1,5},{5,9},{9,13},{2,6},{6,10},{10,14},{3,7},{... | collective-permute-start | bytes 196616 | tf_op jit(solution)/shard_map/ppermute | solution.py:17
  190.6 5.5 %collective-permute-start.10 = (bf16[128,256]{1,0:T(8,128)(2,1)S(1)}, bf16[128,256]{1,0:T(8,128)(2,1)S(1)}, u32[]{:S(2)}, u32[]{:S(2)}) collective-permute-start(bf16[128,256]{1,0:T(8,128)(2,1)S(1)} %get-tuple-element.21), channel_id=1, source_target_pairs={{0,8},{4,12},{1,9},{5,13},{2,10},{6,14},{3,11},{7,15},{16,24},{20,... | collective-permute-start | bytes 196616 | tf_op jit(solution)/shard_map/ppermute | solution.py:17
  197.4 2.5 fusion.7
  200.0 3.1 collective-permute-done.11
  203.2 32.9 %gather_fusion.8 = bf16[8192,256]{1,0:T(8,128)(2,1)} fusion(bf16[768,256]{1,0:T(8,128)(2,1)S(1)} %pad_maximum_fusion.1, s32[8192]{0:T(1024)S(1)} %copy-done.6), kind=kCustom, calls=%fused_computation.3.clone | custom fusion | bytes 8421376 | tf_op jit(solution)/shard_map/jit(_take)/gather | solution.py:158
  236.1 3.6 %broadcast_select_fusion = bf16[32,256,256]{2,1,0:T(8,128)(2,1)S(1)} fusion(bf16[32,256,256]{2,1,0:T(8,128)(2,1)} %bitcast.191, pred[32,256]{1,0:T(8,128)(4,1)S(1)} %compare_and_fusion), kind=kLoop, calls=%fused_computation.11 | loop fusion | flops 2097152 | bytes 8396800 | tf_op jit(solution)/shard_map/jit(_take)/select_n | solution.py:158
  242.9 1.9 fusion.5
  245.6 29.5 %all-reduce.9.cloned.1.call-done = bf16[256,512]{1,0:T(8,128)(2,1)} async-done(((bf16[256,512]{1,0:T(8,128)(2,1)}), bf16[256,512]{1,0:T(8,128)(2,1)}) %all-reduce.9.cloned.1.call-update) | async-done | bytes 262160 | tf_op jit(solution)/shard_map/psum | solution.py:45
  280.2 3.4 %collective-permute-start.12 = (bf16[128,128]{1,0:T(8,128)(2,1)S(1)}, bf16[128,128]{1,0:T(8,128)(2,1)S(1)}, u32[]{:S(2)}, u32[]{:S(2)}) collective-permute-start(bf16[128,128]{1,0:T(8,128)(2,1)S(1)} %get-tuple-element.34), channel_id=1, source_target_pairs={{0,4},{4,8},{8,12},{1,5},{5,9},{9,13},{2,6},{6,10},{10,14},{3,7},{... | collective-permute-start | bytes 98312 | tf_op jit(solution)/shard_map/ppermute | solution.py:17
  284.9 5.5 %collective-permute-start.14 = (bf16[128,128]{1,0:T(8,128)(2,1)S(1)}, bf16[128,128]{1,0:T(8,128)(2,1)S(1)}, u32[]{:S(2)}, u32[]{:S(2)}) collective-permute-start(bf16[128,128]{1,0:T(8,128)(2,1)S(1)} %get-tuple-element.32), channel_id=1, source_target_pairs={{0,8},{4,12},{1,9},{5,13},{2,10},{6,14},{3,11},{7,15},{16,24},{20,... | collective-permute-start | bytes 98312 | tf_op jit(solution)/shard_map/ppermute | solution.py:17
  292.0 5.1 %collective-permute-done.15 = bf16[128,128]{1,0:T(8,128)(2,1)S(1)} collective-permute-done((bf16[128,128]{1,0:T(8,128)(2,1)S(1)}, bf16[128,128]{1,0:T(8,128)(2,1)S(1)}, u32[]{:S(2)}, u32[]{:S(2)}) %collective-permute-start.15) | collective-permute-done | bytes 32800 | tf_op jit(solution)/shard_map/ppermute | solution.py:17
  297.1 3.2 gather_fusion.4
  301.5 28.8 %all-reduce.11.cloned.1.call-done = bf16[84,512]{1,0:T(8,128)(2,1)} async-done(((bf16[84,512]{1,0:T(8,128)(2,1)}), bf16[84,512]{1,0:T(8,128)(2,1)}) %all-reduce.11.cloned.1.call-update) | async-done | bytes 86032 | tf_op jit(solution)/shard_map/psum | solution.py:204
  330.4 1.5 copy.86
  (195 shorter events, 48.1 us)
Async XLA Ops:
  6.5 77.2 %all-reduce.5.cloned.1.call-start = ((), (), s32[]{:S(2)}) async-start(), calls=%async_computation | async-start | bytes 524288 | tf_op jit(solution)/shard_map/psum | solution.py:45
  8.7 21.6 %copy-start.3 = (bf16[2,512,3,128]{3,1,2,0:T(8,128)(2,1)S(1)}, bf16[2,512,3,128]{3,1,2,0:T(8,128)(2,1)}, u32[]{:S(2)}) copy-start(bf16[2,512,3,128]{3,1,2,0:T(8,128)(2,1)} %param.43) | copy-start | bytes 2359300
  15.2 23.8 %collective-permute-start = (bf16[256,128]{1,0:T(8,128)(2,1)}, bf16[256,128]{1,0:T(8,128)(2,1)}, u32[]{:S(2)}, u32[]{:S(2)}) collective-permute-start(bf16[256,128]{1,0:T(8,128)(2,1)} %get-tuple-element.30), channel_id=1, source_target_pairs={{0,4},{4,8},{8,12},{1,5},{5,9},{9,13},{2,6},{6,10},{10,14},{3,7},{... | collective-permute-start | bytes 196616 | tf_op jit(solution)/shard_map/ppermute | solution.py:17
  20.8 19.1 %collective-permute-start.1 = (bf16[256,128]{1,0:T(8,128)(2,1)}, bf16[256,128]{1,0:T(8,128)(2,1)}, u32[]{:S(2)}, u32[]{:S(2)}) collective-permute-start(bf16[256,128]{1,0:T(8,128)(2,1)} %get-tuple-element.29), channel_id=1, source_target_pairs={{4,0},{8,4},{12,8},{5,1},{9,5},{13,9},{6,2},{10,6},{14,10},{7,3},{... | collective-permute-start | bytes 196616 | tf_op jit(solution)/shard_map/ppermute | solution.py:17
  22.1 18.7 %collective-permute-start.2 = (bf16[256,128]{1,0:T(8,128)(2,1)}, bf16[256,128]{1,0:T(8,128)(2,1)}, u32[]{:S(2)}, u32[]{:S(2)}) collective-permute-start(bf16[256,128]{1,0:T(8,128)(2,1)} %get-tuple-element.28), channel_id=1, source_target_pairs={{0,8},{4,12},{1,9},{5,13},{2,10},{6,14},{3,11},{7,15},{16,24},{20,... | collective-permute-start | bytes 196616 | tf_op jit(solution)/shard_map/ppermute | solution.py:17
  27.6 14.0 %collective-permute-start.3 = (bf16[256,128]{1,0:T(8,128)(2,1)}, bf16[256,128]{1,0:T(8,128)(2,1)}, u32[]{:S(2)}, u32[]{:S(2)}) collective-permute-start(bf16[256,128]{1,0:T(8,128)(2,1)} %get-tuple-element.27), channel_id=1, source_target_pairs={{8,0},{12,4},{9,1},{13,5},{10,2},{14,6},{11,3},{15,7},{24,16},{28,... | collective-permute-start | bytes 196616 | tf_op jit(solution)/shard_map/ppermute | solution.py:17
  30.3 76.8 %copy-start.5 = (s32[8192]{0:T(1024)}, s32[8192]{0:T(1024)S(1)}, u32[]{:S(2)}) copy-start(s32[8192]{0:T(1024)S(1)} %broadcast_clamp_fusion) | copy-start | bytes 98308
  39.0 47.0 %copy-start.22 = (f32[1,512]{1,0:T(1,128)S(1)}, f32[1,512]{1,0:T(1,128)}, u32[]{:S(2)}) copy-start(f32[1,512]{1,0:T(1,128)} %get-tuple-element.36) | copy-start | bytes 6148
  45.7 42.0 %copy-start.17 = (s32[1024]{0:T(1024)S(1)}, s32[1024]{0:T(1024)}, u32[]{:S(2)}) copy-start(s32[1024]{0:T(1024)} %get-tuple-element.45) | copy-start | bytes 12292
  48.2 53.2 %copy-start.32 = (bf16[2,512,512]{2,1,0:T(8,128)(2,1)S(1)}, bf16[2,512,512]{2,1,0:T(8,128)(2,1)}, u32[]{:S(2)}) copy-start(bf16[2,512,512]{2,1,0:T(8,128)(2,1)} %param.48) | copy-start | bytes 3145732
  48.2 131.8 %all-reduce.7.cloned.1.call-start = ((), (), s32[]{:S(2)}) async-start(), calls=%async_computation.1 | async-start | bytes 524288 | tf_op jit(solution)/shard_map/psum | solution.py:45
  48.3 55.6 %copy-start.26 = (pred[4,128]{1,0:T(4,128)(4,1)}, pred[4,128]{1,0:T(4,128)(4,1)S(1)}, u32[]{:S(2)}) copy-start(pred[4,128]{1,0:T(4,128)(4,1)S(1)} %compare_and_fusion.5) | copy-start | bytes 1540
  89.8 14.8 %collective-permute-start.4 = (bf16[128,256]{1,0:T(8,128)(2,1)S(1)}, bf16[128,256]{1,0:T(8,128)(2,1)S(1)}, u32[]{:S(2)}, u32[]{:S(2)}) collective-permute-start(bf16[128,256]{1,0:T(8,128)(2,1)S(1)} %get-tuple-element.23), channel_id=1, source_target_pairs={{0,4},{4,8},{8,12},{1,5},{5,9},{9,13},{2,6},{6,10},{10,14},{3,7},{... | collective-permute-start | bytes 196616 | tf_op jit(solution)/shard_map/ppermute | solution.py:17
  93.2 11.4 %collective-permute-start.5 = (bf16[128,256]{1,0:T(8,128)(2,1)S(1)}, bf16[128,256]{1,0:T(8,128)(2,1)S(1)}, u32[]{:S(2)}, u32[]{:S(2)}) collective-permute-start(bf16[128,256]{1,0:T(8,128)(2,1)S(1)} %get-tuple-element.26), channel_id=1, source_target_pairs={{4,0},{8,4},{12,8},{5,1},{9,5},{13,9},{6,2},{10,6},{14,10},{7,3},{... | collective-permute-start | bytes 196616 | tf_op jit(solution)/shard_map/ppermute | solution.py:17
  94.5 10.1 %collective-permute-start.6 = (bf16[128,256]{1,0:T(8,128)(2,1)S(1)}, bf16[128,256]{1,0:T(8,128)(2,1)S(1)}, u32[]{:S(2)}, u32[]{:S(2)}) collective-permute-start(bf16[128,256]{1,0:T(8,128)(2,1)S(1)} %get-tuple-element.25), channel_id=1, source_target_pairs={{0,8},{4,12},{1,9},{5,13},{2,10},{6,14},{3,11},{7,15},{16,24},{20,... | collective-permute-start | bytes 196616 | tf_op jit(solution)/shard_map/ppermute | solution.py:17
  100.0 7.1 %collective-permute-start.7 = (bf16[128,256]{1,0:T(8,128)(2,1)S(1)}, bf16[128,256]{1,0:T(8,128)(2,1)S(1)}, u32[]{:S(2)}, u32[]{:S(2)}) collective-permute-start(bf16[128,256]{1,0:T(8,128)(2,1)S(1)} %get-tuple-element.24), channel_id=1, source_target_pairs={{8,0},{12,4},{9,1},{13,5},{10,2},{14,6},{11,3},{15,7},{24,16},{28,... | collective-permute-start | bytes 196616 | tf_op jit(solution)/shard_map/ppermute | solution.py:17
  147.3 36.5 %copy-start.18 = (s32[1024]{0:T(1024)S(1)}, s32[1024]{0:T(1024)}, u32[]{:S(2)}) copy-start(s32[1024]{0:T(1024)} %get-tuple-element.45) | copy-start | bytes 12292
  147.3 38.5 %copy-start.27 = (pred[4,128]{1,0:T(4,128)(4,1)S(1)}, pred[4,128]{1,0:T(4,128)(4,1)}, u32[]{:S(2)}) copy-start(pred[4,128]{1,0:T(4,128)(4,1)} %copy-done.26) | copy-start | bytes 1540
  149.2 48.2 %copy-start.21 = (f32[1,512]{1,0:T(1,128)S(1)}, f32[1,512]{1,0:T(1,128)}, u32[]{:S(2)}) copy-start(f32[1,512]{1,0:T(1,128)} %get-tuple-element.35) | copy-start | bytes 6148
  149.2 48.2 %copy-start.33 = (bf16[2,512,512]{2,1,0:T(8,128)(2,1)S(1)}, bf16[2,512,512]{2,1,0:T(8,128)(2,1)}, u32[]{:S(2)}) copy-start(bf16[2,512,512]{2,1,0:T(8,128)(2,1)} %param.48) | copy-start | bytes 3145732
  149.2 125.9 %all-reduce.9.cloned.1.call-start = ((), (), s32[]{:S(2)}) async-start(), calls=%async_computation.2 | async-start | bytes 524288 | tf_op jit(solution)/shard_map/psum | solution.py:45
  185.9 14.1 %collective-permute-start.8 = (bf16[128,256]{1,0:T(8,128)(2,1)S(1)}, bf16[128,256]{1,0:T(8,128)(2,1)S(1)}, u32[]{:S(2)}, u32[]{:S(2)}) collective-permute-start(bf16[128,256]{1,0:T(8,128)(2,1)S(1)} %get-tuple-element.19), channel_id=1, source_target_pairs={{0,4},{4,8},{8,12},{1,5},{5,9},{9,13},{2,6},{6,10},{10,14},{3,7},{... | collective-permute-start | bytes 196616 | tf_op jit(solution)/shard_map/ppermute | solution.py:17
  189.3 10.7 %collective-permute-start.9 = (bf16[128,256]{1,0:T(8,128)(2,1)S(1)}, bf16[128,256]{1,0:T(8,128)(2,1)S(1)}, u32[]{:S(2)}, u32[]{:S(2)}) collective-permute-start(bf16[128,256]{1,0:T(8,128)(2,1)S(1)} %get-tuple-element.22), channel_id=1, source_target_pairs={{4,0},{8,4},{12,8},{5,1},{9,5},{13,9},{6,2},{10,6},{14,10},{7,3},{... | collective-permute-start | bytes 196616 | tf_op jit(solution)/shard_map/ppermute | solution.py:17
  190.6 9.4 %collective-permute-start.10 = (bf16[128,256]{1,0:T(8,128)(2,1)S(1)}, bf16[128,256]{1,0:T(8,128)(2,1)S(1)}, u32[]{:S(2)}, u32[]{:S(2)}) collective-permute-start(bf16[128,256]{1,0:T(8,128)(2,1)S(1)} %get-tuple-element.21), channel_id=1, source_target_pairs={{0,8},{4,12},{1,9},{5,13},{2,10},{6,14},{3,11},{7,15},{16,24},{20,... | collective-permute-start | bytes 196616 | tf_op jit(solution)/shard_map/ppermute | solution.py:17
  196.1 7.1 %collective-permute-start.11 = (bf16[128,256]{1,0:T(8,128)(2,1)S(1)}, bf16[128,256]{1,0:T(8,128)(2,1)S(1)}, u32[]{:S(2)}, u32[]{:S(2)}) collective-permute-start(bf16[128,256]{1,0:T(8,128)(2,1)S(1)} %get-tuple-element.20), channel_id=1, source_target_pairs={{8,0},{12,4},{9,1},{13,5},{10,2},{14,6},{11,3},{15,7},{24,16},{28,... | collective-permute-start | bytes 196616 | tf_op jit(solution)/shard_map/ppermute | solution.py:17
  244.8 55.5 %copy-start.20 = (pred[3,512]{1,0:T(4,128)(4,1)S(1)}, pred[3,512]{1,0:T(4,128)(4,1)}, u32[]{:S(2)}) copy-start(pred[3,512]{1,0:T(4,128)(4,1)} %compare_and_fusion.1) | copy-start | bytes 4612
  244.8 85.5 %all-reduce.11.cloned.1.call-start = ((), (), s32[]{:S(2)}) async-start(), calls=%async_computation.3 | async-start | bytes 180224 | tf_op jit(solution)/shard_map/psum | solution.py:204
  276.2 24.4 %copy-start.12 = (bf16[128,84]{0,1:T(8,128)(2,1)S(1)}, bf16[128,84]{0,1:T(8,128)(2,1)}, u32[]{:S(2)}) copy-start(bf16[128,84]{0,1:T(8,128)(2,1)} %param.53) | copy-start | bytes 64516
  280.2 11.5 %collective-permute-start.12 = (bf16[128,128]{1,0:T(8,128)(2,1)S(1)}, bf16[128,128]{1,0:T(8,128)(2,1)S(1)}, u32[]{:S(2)}, u32[]{:S(2)}) collective-permute-start(bf16[128,128]{1,0:T(8,128)(2,1)S(1)} %get-tuple-element.34), channel_id=1, source_target_pairs={{0,4},{4,8},{8,12},{1,5},{5,9},{9,13},{2,6},{6,10},{10,14},{3,7},{... | collective-permute-start | bytes 98312 | tf_op jit(solution)/shard_map/ppermute | solution.py:17
  283.6 8.1 %collective-permute-start.13 = (bf16[128,128]{1,0:T(8,128)(2,1)S(1)}, bf16[128,128]{1,0:T(8,128)(2,1)S(1)}, u32[]{:S(2)}, u32[]{:S(2)}) collective-permute-start(bf16[128,128]{1,0:T(8,128)(2,1)S(1)} %get-tuple-element.33), channel_id=1, source_target_pairs={{4,0},{8,4},{12,8},{5,1},{9,5},{13,9},{6,2},{10,6},{14,10},{7,3},{... | collective-permute-start | bytes 98312 | tf_op jit(solution)/shard_map/ppermute | solution.py:17
  284.9 7.1 %collective-permute-start.14 = (bf16[128,128]{1,0:T(8,128)(2,1)S(1)}, bf16[128,128]{1,0:T(8,128)(2,1)S(1)}, u32[]{:S(2)}, u32[]{:S(2)}) collective-permute-start(bf16[128,128]{1,0:T(8,128)(2,1)S(1)} %get-tuple-element.32), channel_id=1, source_target_pairs={{0,8},{4,12},{1,9},{5,13},{2,10},{6,14},{3,11},{7,15},{16,24},{20,... | collective-permute-start | bytes 98312 | tf_op jit(solution)/shard_map/ppermute | solution.py:17
  290.4 6.7 %collective-permute-start.15 = (bf16[128,128]{1,0:T(8,128)(2,1)S(1)}, bf16[128,128]{1,0:T(8,128)(2,1)S(1)}, u32[]{:S(2)}, u32[]{:S(2)}) collective-permute-start(bf16[128,128]{1,0:T(8,128)(2,1)S(1)} %get-tuple-element.31), channel_id=1, source_target_pairs={{8,0},{12,4},{9,1},{13,5},{10,2},{14,6},{11,3},{15,7},{24,16},{28,... | collective-permute-start | bytes 98312 | tf_op jit(solution)/shard_map/ppermute | solution.py:17
  (23 other events, 326.2 us)
Sparse Core Ops, SparseCore 0:
  48.3 35.3 all-reduce.4
  149.4 30.6 all-reduce.6
  244.9 30.1 all-reduce.8
  301.7 28.6 all-reduce.10
where the time goes:
time: 340 us; the launch traced here: 338 us
  waiting for transfers between devices  135 us (40%)
  local copies, waits for them, and re-layouts  95.5 us (28%)
  starting transfers between devices  48.3 us (14%)
  other arithmetic  23.4 us (7%)
  matrix products  22.3 us (7%)
  between operations  14.2 us (4%)
    psum x3, waiting for transfers between devices, width_total(): return lax.psum(partial_term.astype(jnp.bfloat16), 'mp').astype(jnp.float32)  94.9 us
    gather x2, local copies, waits for them, and re-layouts, shards(): selected_entries = jnp.take(halo_table, neighbours[0], axis=0)  65.8 us
    ppermute x16, starting transfers between devices, passed_along(): lax.ppermute(value, axis, [(source, source + steps) for source in range(i...  48 us
    psum x1, waiting for transfers between devices, shards(): return lax.psum(output_term.astype(jnp.bfloat16), 'mp')  28.8 us
    ppermute x16, waiting for transfers between devices, passed_along(): lax.ppermute(value, axis, [(source, source + steps) for source in range(i...  11 us
    select_n x2, other arithmetic, shards(): selected_entries = jnp.take(halo_table, neighbours[0], axis=0)  7.16 us
  transfers between devices with their start and end apart: 20, of which 8 were waited for; matrix products, arithmetic and copies ran while one was open for 6% of the time, Pallas kernels for 0%

commit v1 on v0

v1 whole, which is shorter than its diff:
```python
import functools
import math

import jax
import jax.numpy as jnp
from jax import lax
from jax.experimental import pallas as pl
from jax.experimental.pallas import tpu as pltpu
from jax.sharding import PartitionSpec as P

LAYERS = 2
EPSILON = 1e-05
LANES = 128
MESH = pl.DeviceIdType.MESH
BF16 = jnp.bfloat16
F32 = jnp.float32


def offset_of(number):
    return (number // 2 + 1) * (1 if number % 2 == 0 else -1)


def silu(x):
    half = 0.5 * x
    return half + half * jnp.tanh(half)


def dot(a, b):
    return jnp.dot(a, b, preferred_element_type=F32)


def layer_norm(values, gain):
    average = jnp.mean(values, axis=-1, keepdims=True)
    centred = values - average
    spread = jnp.mean(centred * centred, axis=-1, keepdims=True)
    return centred * lax.rsqrt(spread + EPSILON) * gain


def rms_scale(values, gain):
    return values * lax.rsqrt(jnp.mean(values * values, axis=-1, keepdims=True) + EPSILON) * gain


def column(row):
    return jnp.transpose(jnp.broadcast_to(row, (LANES, row.shape[1])))


def fill_one_hot(ref, at, row, first, count):
    col = column(row)
    lane = lax.broadcasted_iota(jnp.int32, col.shape, 1)
    rows = row.shape[1]
    for block in range(count // LANES):
        hit = col == lane + (first + block * LANES)
        ref[at : at + rows, block * LANES : (block + 1) * LANES] = jnp.where(hit, 1.0, 0.0).astype(
            BF16
        )


def kernel(
    patches,
    grid_in,
    mesh_static,
    embed_weight,
    embed_bias,
    encode_source,
    encode_target,
    encode_edge,
    encode_bias,
    encode_out,
    layer_gain,
    attention_in_hbm,
    query_gain,
    key_gain,
    attention_out_hbm,
    hidden_in_hbm,
    hidden_out_hbm,
    final_gain,
    decode_node_hbm,
    decode_grid_hbm,
    decode_bias,
    decode_out,
    cell_lists,
    edge_source,
    edge_target,
    edge_geometry,
    halo_lists,
    neighbours,
    node_lists,
    cell_nodes,
    out,
    attention_in,
    attention_out,
    hidden_in,
    hidden_out,
    decode_node,
    decode_grid,
    latent_grid,
    cell_hot,
    cell_send,
    cell_table,
    source_hot,
    pre,
    node_hot,
    halo_hot,
    counts,
    part_send,
    part_recv,
    half_send,
    half_recv,
    normed,
    latent,
    key_send,
    key_table,
    list_hot,
    node_send,
    node_table,
    choose_hot,
    grid_part,
    out_send,
    out_recv,
    load_sem,
    cell_ssem,
    cell_rsem,
    key_ssem,
    key_rsem,
    node_ssem,
    node_rsem,
    sum_ssem,
    sum_rsem,
    out_ssem,
    out_rsem,
):
    p = lax.axis_index("patch")
    m = lax.axis_index("mp")
    near = cell_lists.shape[1]
    side = m % 2
    sibling = m + 1 - 2 * side
    across = (m + 2) % 4

    loads = [
        pltpu.make_async_copy(src, dst, load_sem.at[i])
        for i, (src, dst) in enumerate(
            [
                (attention_in_hbm, attention_in),
                (hidden_in_hbm, hidden_in),
                (hidden_out_hbm, hidden_out),
                (attention_out_hbm, attention_out),
                (decode_grid_hbm, decode_grid),
                (decode_node_hbm, decode_node),
            ]
        )
    ]
    for load in loads:
        load.start()

    def has_dst(k):
        b = offset_of(k)
        return p + b < patches if b > 0 else p + b >= 0

    def has_src(k):
        b = offset_of(k)
        return p - b >= 0 if b > 0 else p - b < patches

    barrier = pltpu.get_barrier_semaphore()
    for partner in (sibling, across):
        pl.semaphore_signal(barrier, inc=1, device_id={"mp": partner}, device_id_type=MESH)
    for k in range(near):

        @pl.when(has_dst(k))
        def _(k=k):
            pl.semaphore_signal(
                barrier, inc=1, device_id={"patch": p + offset_of(k)}, device_id_type=MESH
            )

    nodes = mesh_static.shape[0]
    cells = latent_grid.shape[0]
    width = encode_source.shape[1]
    cap_cell = cell_lists.shape[2]
    cap_key = halo_lists.shape[2]
    cap_node = node_lists.shape[2]
    half = nodes // 2

    for k in range(near):

        @pl.when(jnp.logical_not(has_src(k)))
        def _(k=k):
            cell_table[k] = jnp.zeros(cell_table.shape[1:], BF16)
            for layer in range(LAYERS):
                key_table[layer, k + 1] = jnp.zeros(key_table.shape[2:], BF16)
            node_table[k + 1] = jnp.zeros(node_table.shape[1:], BF16)

    channel_dims = (((0,), (0,)), ((), ()))
    latent_grid[...] = silu(
        lax.dot_general(grid_in[...], embed_weight[...], channel_dims, preferred_element_type=F32)
        + embed_bias[...][None, :]
    ).astype(BF16)
    projected = dot(latent_grid[...], encode_source[...]).astype(BF16)

    for k in range(near):
        fill_one_hot(cell_hot, k * cap_cell, cell_lists[0, k : k + 1, :], 0, cells)
    cell_send[...] = (
        dot(cell_hot[...], projected).astype(BF16).reshape(near, cap_cell, width)
    )

    peers = 2
    for k in range(near):
        peers = peers + jnp.where(has_src(k), 1, 0)
    pl.semaphore_wait(barrier, peers)

    def passes(send, recv, ssem, rsem):
        return [
            pltpu.make_async_remote_copy(
                src_ref=send(k),
                dst_ref=recv(k),
                send_sem=ssem(k),
                recv_sem=rsem(k),
                device_id={"patch": p + offset_of(k)},
                device_id_type=MESH,
            )
            for k in range(near)
        ]

    def start_all(copies):
        for k in range(near):

            @pl.when(has_dst(k))
            def _(k=k):
                copies[k].start()

    def arrive_all(copies):
        for k in range(near):

            @pl.when(has_src(k))
            def _(k=k):
                copies[k].wait_recv()

    def sent_all(copies):
        for k in range(near):

            @pl.when(has_dst(k))
            def _(k=k):
                copies[k].wait_send()

    cell_copies = passes(
        lambda k: cell_send.at[k],
        lambda k: cell_table.at[k],
        lambda k: cell_ssem.at[k],
        lambda k: cell_rsem.at[k],
    )
    start_all(cell_copies)

    edges = edge_source.shape[1]
    sources = edge_source[0:1, :]
    fill_one_hot(source_hot, 0, sources, 0, source_hot.shape[1])
    targets = edge_target[0:1, :]
    target_part = dot(mesh_static[...], encode_target[...]).astype(BF16)
    geometry_term = lax.dot_general(
        edge_geometry[0], encode_edge[...], channel_dims, preferred_element_type=F32
    )
    fill_one_hot(node_hot, 0, targets, 0, nodes)
    pre[...] = (
        dot(node_hot[...], target_part)
        + geometry_term
        + encode_bias[...][None, :]
        + dot(source_hot[:, :cells], projected)
    )
    gather_hot = jnp.where(
        lax.broadcasted_iota(jnp.int32, (nodes, edges), 0) == targets, 1.0, 0.0
    ).astype(BF16)
    node_rows = lax.broadcasted_iota(jnp.int32, (LANES, nodes), 0)

    arrive_all(cell_copies)
    messages = silu(
        pre[...]
        + dot(source_hot[:, cells:], cell_table[...].reshape(near * cap_cell, width))
    ).astype(BF16)
    gathered = dot(gather_hot, messages).astype(BF16)
    part = dot(gathered, encode_out[...])

    own = pl.multiple_of(side * half, half)
    other = pl.multiple_of((1 - side) * half, half)
    pending = []

    def to_partner(src, dst, at, stage, partner):
        return pltpu.make_async_remote_copy(
            src_ref=src,
            dst_ref=dst,
            send_sem=sum_ssem.at[at, stage],
            recv_sem=sum_rsem.at[at, stage],
            device_id={"mp": partner},
            device_id_type=MESH,
        )

    def add_and_norm(at, part, gain, filler):
        part_send[at] = part.astype(BF16)
        first = to_partner(
            part_send.at[at, pl.ds(other, half)], part_recv.at[at], at, 0, sibling
        )
        first.start()
        first.wait_recv()
        pair = part_send[at, pl.ds(own, half)].astype(F32) + part_recv[at].astype(F32)
        half_send[at] = pair.astype(BF16)
        second = to_partner(half_send.at[at], half_recv.at[at], at, 1, across)
        second.start()
        filler()
        base = mesh_static[pl.ds(own, half)].astype(F32) if at == 0 else latent[...]
        second.wait_recv()
        total = base + (half_send[at].astype(F32) + half_recv[at].astype(F32))
        if at < LAYERS:
            latent[...] = total
        normed[at, pl.ds(own, half)] = layer_norm(total, gain).astype(BF16)
        third = to_partner(
            normed.at[at, pl.ds(own, half)], normed.at[at, pl.ds(own, half)], at, 2, sibling
        )
        third.start()
        back = to_partner(
            normed.at[at, pl.ds(other, half)], normed.at[at, pl.ds(other, half)], at, 2, sibling
        )
        back.wait_recv()
        pending.extend([first, second, third])

    def prepare_attention():
        for k in range(near):
            fill_one_hot(halo_hot, k * cap_key, halo_lists[0, k : k + 1, :], 0, nodes)
        for block in range(counts.shape[1] // LANES):
            total = jnp.zeros((LANES, nodes), F32)
            rows = node_rows + block * LANES
            for n in range(neighbours.shape[1]):
                total = total + jnp.where(rows == neighbours[0, n : n + 1, :], 1.0, 0.0)
            counts[:, block * LANES : (block + 1) * LANES] = jnp.transpose(total)

    def prepare_decode():
        loads[4].wait()
        loads[5].wait()
        grid_part[...] = dot(latent_grid[...], decode_grid[...]) + decode_bias[...][None, :]
        for k in range(near):
            fill_one_hot(list_hot, k * cap_node, node_lists[0, k : k + 1, :], 0, nodes)

    def prepare_choice():
        for j in range(3):
            fill_one_hot(choose_hot, j * cells, cell_nodes[j : j + 1, :], 0, choose_hot.shape[1])

    fillers = [prepare_attention, prepare_decode, prepare_choice]
    add_and_norm(0, part, layer_gain[0:1, :], fillers[0])

    node_copies_key = []
    for layer in range(LAYERS):
        if layer == 0:
            loads[0].wait()
        rows = normed[layer]
        projections = dot(rows, attention_in[layer])
        queries = rms_scale(projections[:, :width], query_gain[layer : layer + 1, :]).astype(BF16)
        keys = rms_scale(projections[:, width : 2 * width], key_gain[layer : layer + 1, :]).astype(
            BF16
        )
        values = projections[:, 2 * width :].astype(BF16)
        key_value = jnp.concatenate([keys, values], axis=1)
        key_send[layer] = (
            dot(halo_hot[...], key_value).astype(BF16).reshape(near, cap_key, 2 * width)
        )
        copies = passes(
            lambda k: key_send.at[layer, k],
            lambda k: key_table.at[layer, k + 1],
            lambda k: key_ssem.at[layer, k],
            lambda k: key_rsem.at[layer, k],
        )
        start_all(copies)
        node_copies_key.append(copies)
        if layer == 0:
            for load in loads[1:4]:
                load.wait()
        hidden = silu(dot(rows, hidden_in[layer])).astype(BF16)
        part = dot(hidden, hidden_out[layer])
        last = (((1,), (1,)), ((), ()))
        scale = 1.0 / math.sqrt(width)
        near_weights = (
            jnp.exp(lax.dot_general(queries, keys, last, preferred_element_type=F32) * scale)
            * counts[:, :nodes]
        )
        arrive_all(copies)
        far = key_table[layer, 1:].reshape(near * cap_key, 2 * width)
        far_weights = (
            jnp.exp(
                lax.dot_general(queries, far[:, :width], last, preferred_element_type=F32) * scale
            )
            * counts[:, nodes:]
        )
        share = 1.0 / (
            jnp.sum(near_weights, axis=1, keepdims=True)
            + jnp.sum(far_weights, axis=1, keepdims=True)
        )
        attended = (
            dot((near_weights * share).astype(BF16), values)
            + dot((far_weights * share).astype(BF16), far[:, width:])
        ).astype(BF16)
        part = part + dot(attended, attention_out[layer])
        gain = layer_gain[layer + 1 : layer + 2, :] if layer + 1 < LAYERS else final_gain[...][None, :]
        add_and_norm(layer + 1, part, gain, fillers[layer + 1])

    node_part = dot(normed[LAYERS], decode_node[...]).astype(BF16)
    node_send[...] = dot(list_hot[...], node_part).astype(BF16).reshape(near, cap_node, width)
    node_copies = passes(
        lambda k: node_send.at[k],
        lambda k: node_table.at[k + 1],
        lambda k: node_ssem.at[k],
        lambda k: node_rsem.at[k],
    )
    start_all(node_copies)
    chosen_near = dot(choose_hot[:, :nodes], node_part)
    arrive_all(node_copies)
    chosen = chosen_near + dot(
        choose_hot[:, nodes:], node_table[1:].reshape(near * cap_node, width)
    )
    activity = silu(chosen[:cells] + grid_part[...])
    for j in range(1, 3):
        activity = activity + silu(chosen[j * cells : (j + 1) * cells] + grid_part[...])
    channels = decode_out.shape[1]
    term = lax.dot_general(
        decode_out[...],
        activity.astype(BF16),
        (((0,), (1,)), ((), ())),
        preferred_element_type=F32,
    )
    padding = out_send.shape[1] - channels
    out_copies = []
    for stage, partner in enumerate((sibling, across)):
        out_send[stage, :channels] = term.astype(BF16)
        if padding:
            out_send[stage, channels:] = jnp.zeros((padding, cells), BF16)
        copy = pltpu.make_async_remote_copy(
            src_ref=out_send.at[stage],
            dst_ref=out_recv.at[stage],
            send_sem=out_ssem.at[stage],
            recv_sem=out_rsem.at[stage],
            device_id={"mp": partner},
            device_id_type=MESH,
        )
        copy.start()
        out_copies.append(copy)
        copy.wait_recv()
        term = out_send[stage, :channels].astype(F32) + out_recv[stage, :channels].astype(F32)
    out[...] = term.astype(BF16)

    for copies in [cell_copies, node_copies] + node_copies_key:
        sent_all(copies)
    for copy in pending + out_copies:
        copy.wait_send()


def shards(patches, *operands):
    operands = list(operands)
    (grid_in, mesh_static, embed_weight) = operands[:3]
    attention_in = operands[10]
    layers, depth, kinds, width = attention_in.shape
    operands[10] = attention_in.reshape(layers, depth, kinds * width)
    attention_out, hidden_in, hidden_out = operands[13:16]
    decode_node, decode_grid = operands[17:19]
    cell_lists, edge_source = operands[21:23]
    halo_lists, neighbours, node_lists, cell_nodes = operands[25:29]
    channels, cells = grid_in.shape
    nodes, features = mesh_static.shape
    near, cap_cell = cell_lists.shape[1:]
    cap_key = halo_lists.shape[2]
    cap_node = node_lists.shape[2]
    edges = edge_source.shape[1]
    half = nodes // 2
    padded = -(-channels // 16) * 16
    sums = layers + 1
    vmem, dma = pltpu.VMEM, pltpu.SemaphoreType.DMA
    scratch = [
        vmem(operands[10].shape, BF16),
        vmem(attention_out.shape, BF16),
        vmem(hidden_in.shape, BF16),
        vmem(hidden_out.shape, BF16),
        vmem(decode_node.shape, BF16),
        vmem(decode_grid.shape, BF16),
        vmem((cells, features), BF16),
        vmem((near * cap_cell, cells), BF16),
        vmem((near, cap_cell, width), BF16),
        vmem((near, cap_cell, width), BF16),
        vmem((edges, cells + near * cap_cell), BF16),
        vmem((edges, width), F32),
        vmem((edges, nodes), BF16),
        vmem((near * cap_key, nodes), BF16),
        vmem((nodes, nodes + near * cap_key), F32),
        vmem((sums, nodes, features), BF16),
        vmem((sums, half, features), BF16),
        vmem((sums, half, features), BF16),
        vmem((sums, half, features), BF16),
        vmem((sums, nodes, features), BF16),
        vmem((half, features), F32),
        vmem((layers, near, cap_key, 2 * width), BF16),
        vmem((layers, near + 1, cap_key, 2 * width), BF16),
        vmem((near * cap_node, nodes), BF16),
        vmem((near, cap_node, width), BF16),
        vmem((near + 1, cap_node, width), BF16),
        vmem((3 * cells, nodes + near * cap_node), BF16),
        vmem((cells, width), F32),
        vmem((2, padded, cells), BF16),
        vmem((2, padded, cells), BF16),
        dma((6,)),
        dma((near,)),
        dma((near,)),
        dma((layers, near)),
        dma((layers, near)),
        dma((near,)),
        dma((near,)),
        dma((sums, 3)),
        dma((sums, 3)),
        dma((2,)),
        dma((2,)),
    ]
    in_hbm = (10, 13, 14, 15, 17, 18)
    return pl.pallas_call(
        functools.partial(kernel, patches),
        out_shape=jax.ShapeDtypeStruct((channels, cells), BF16),
        in_specs=[
            pl.BlockSpec(memory_space=pl.ANY if i in in_hbm else pltpu.VMEM)
            for i in range(len(operands))
        ],
        out_specs=pl.BlockSpec(memory_space=pltpu.VMEM),
        scratch_shapes=scratch,
        compiler_params=pltpu.CompilerParams(
            collective_id=0, has_side_effects=True, vmem_limit_bytes=50 * 1024 * 1024
        ),
        name="denoise",
    )(*operands)


def solution(mesh):
    in_specs = (
        P(None, ("ens", "patch")),
        P("patch", None),
        P(),
        P(),
        P(None, "mp"),
        P(None, "mp"),
        P(None, "mp"),
        P("mp"),
        P("mp", None),
        P(),
        P(None, None, None, "mp"),
        P(),
        P(),
        P(None, "mp", None),
        P(None, None, "mp"),
        P(None, "mp", None),
        P(),
        P(None, "mp"),
        P(None, "mp"),
        P("mp"),
        P("mp", None),
        P("patch", None, None),
        P("patch", None),
        P("patch", None),
        P("patch", None, None),
        P("patch", None, None),
        P("patch", None, None),
        P("patch", None, None),
        P(None, "patch"),
    )
    out_specs = P(None, ("ens", "patch"))
    return jax.shard_map(
        functools.partial(shards, mesh.shape["patch"]),
        mesh=mesh,
        in_specs=in_specs,
        out_specs=out_specs,
        check_vma=False,
    )
```

time: 340 us -> 64 us (0.19)
  waiting for transfers between devices: 135 us -> 0 us
  local copies, waits for them, and re-layouts: 95.5 us -> 5.32 us
  Pallas kernels: 0 us -> 58.1 us
  starting transfers between devices: 48.3 us -> 0 us
  other arithmetic: 23.4 us -> 0 us
  matrix products: 22.3 us -> 0 us
  between operations: 14.2 us -> 0.35 us
    psum x4 -> x0, waiting for transfers between devices: 124 us -> none  [the longest x3 94.9 us: width_total(): return lax.psum(partial_term.astype(jnp.bfloat16), 'mp').astype(jnp.float32)]
    gather x9 -> x0, local copies, waits for them, and re-layouts: 83.9 us -> none  [the longest x2 65.8 us: shards(): selected_entries = jnp.take(halo_table, neighbours[0], axis=0)]
    pallas_call x0 -> x1, Pallas kernels: none -> 58.1 us  [shards(): pl.pallas_call(functools.partial(kernel, patches), out_shape=jax.ShapeDty...]
    ppermute x16 -> x0, starting transfers between devices: 48 us -> none  [passed_along(): lax.ppermute(value, axis, [(source, source + steps) for source in range(i...]
    dot_general x14 -> x0, matrix products: 19.6 us -> none  [the longest x2 4.98 us: shards(): jnp.dot(hidden, hidden_out[layer_index], preferred_element_type=jnp.float32)]
    ppermute x16 -> x0, waiting for transfers between devices: 11 us -> none  [passed_along(): lax.ppermute(value, axis, [(source, source + steps) for source in range(i...]
    select_n x10 -> x0, other arithmetic: 8.38 us -> none  [the longest x2 7.16 us: shards(): selected_entries = jnp.take(halo_table, neighbours[0], axis=0)]
    reduce_sum x11 -> x0, other arithmetic: 6.34 us -> none  [the longest x3 3.38 us: layer_norm(): average = jnp.mean(values, axis=-1, keepdims=True)]
  transfers between devices with their start and end apart: 20 -> 0, of which waited for: 8 -> 0; matrix products, arithmetic and copies ran while one was open for 6% -> 0% of each run, Pallas kernels for 0% -> 0%
where the time goes in v1:
time: 64 us; the launch traced here: 63.8 us
  Pallas kernels  58.1 us (91%)
  local copies, waits for them, and re-layouts  5.32 us (8%)
    pallas_call x1, Pallas kernels, shards(): pl.pallas_call(functools.partial(kernel, patches), out_shape=jax.ShapeDty...  58.1 us
    unnamed x57, local copies, waits for them, and re-layouts  3.72 us
    reshape x1, local copies, waits for them, and re-layouts, shards(): operands[10] = attention_in.reshape(layers, depth, kinds * width)  1.61 us

profile of v1, /device:TPU:0, one launch (start us, length us, event | category | flops | bytes accessed | tf_op | source)
XLA Modules:
  0.0 63.8 jit_solution(11510154546244691384)
XLA Ops:
  0.0 0.0 copy-start.7
  0.0 0.0 copy-start.8
  0.0 0.0 copy-start.9
  0.0 0.0 copy-start.14
  0.1 0.0 copy-start.15
  0.1 0.0 copy-start.16
  0.1 0.0 copy-start.18
  0.1 0.0 copy-start.19
  0.1 0.0 copy-start.20
  0.1 0.0 copy-start.22
  0.1 0.0 copy-start.23
  0.1 0.0 copy-start.25
  0.1 2.5 %copy.32 = bf16[2,512,3,128]{1,3,2,0:T(8,128)(2,1)} copy(bf16[2,512,3,128]{3,1,2,0:T(8,128)(2,1)} %param.39) | data formatting | bytes 1572864 | tf_op args[10]
  2.6 0.0 copy-start.24
  2.6 1.6 %copy.33.attention_in_hbm = bf16[2,512,384]{2,1,0:T(8,128)(2,1)S(1)} copy(bf16[2,512,384]{1,2,0:T(8,128)(2,1)} %bitcast.1) | data formatting | bytes 1572864 | tf_op jit(solution)/shard_map/reshape | solution.py:454
  4.2 0.0 copy-done.26
  4.2 0.0 copy-start.10
  4.3 0.0 copy-start.11
  4.3 0.0 copy-start.12
  4.3 0.0 copy-start.13
  4.3 0.0 copy-start.17
  4.3 0.1 copy.34.decode_out
  4.4 0.0 copy-done.3
  4.4 0.0 copy-done.4
  4.4 0.0 copy-done.5
  4.5 0.0 copy-done.6
  4.5 0.0 copy-done.7
  4.5 0.0 copy-done.8
  4.6 0.4 copy-done.10
  5.0 0.0 copy-done.12
  5.0 58.1 %denoise.1 = bf16[84,512]{1,0:T(8,128)(2,1)S(1)} custom-call(bf16[84,512]{1,0:T(8,128)(2,1)S(1)} %copy-done.8, bf16[256,512]{1,0:T(8,128)(2,1)S(1)} %copy-done.1, bf16[84,512]{1,0:T(8,128)(2,1)S(1)} %copy-done.9, f32[512]{0:T(512)S(1)} %copy-done.17, bf16[512,128]{1,0:T(8,128)(2,1)S(1)} %copy-done.3, bf16[512,128]{1,0:T(8,128)(2,1)S(1)} %copy-done.4, ...), custom_call_target="tpu_custom_call" | custom-call | tf_op jit(solution)/shard_map/denoise/pallas_call | solution.py:513
  63.1 0.6 %copy.36 = bf16[84,512]{1,0:T(8,128)(2,1)} copy(bf16[84,512]{1,0:T(8,128)(2,1)S(1)} %denoise.1) | data formatting | bytes 172032
  (27 shorter events, 0.1 us)
Async XLA Ops:
  0.0 4.2 %copy-start.26 = (bf16[128,84]{0,1:T(8,128)(2,1)S(1)}, bf16[128,84]{0,1:T(8,128)(2,1)}, u32[]{:S(2)}) copy-start(bf16[128,84]{0,1:T(8,128)(2,1)} %param.49) | copy-start | bytes 64516
  0.0 4.4 %copy-start.3 = (bf16[512,128]{1,0:T(8,128)(2,1)S(1)}, bf16[512,128]{1,0:T(8,128)(2,1)}, u32[]{:S(2)}) copy-start(bf16[512,128]{1,0:T(8,128)(2,1)} %encode_source.1) | copy-start | bytes 393220
  0.0 4.4 %copy-start.4 = (bf16[512,128]{1,0:T(8,128)(2,1)S(1)}, bf16[512,128]{1,0:T(8,128)(2,1)}, u32[]{:S(2)}) copy-start(bf16[512,128]{1,0:T(8,128)(2,1)} %encode_target.1) | copy-start | bytes 393220
  0.0 4.4 %copy-start.5 = (bf16[128,512]{1,0:T(8,128)(2,1)S(1)}, bf16[128,512]{1,0:T(8,128)(2,1)}, u32[]{:S(2)}) copy-start(bf16[128,512]{1,0:T(8,128)(2,1)} %encode_out.1) | copy-start | bytes 393220
  0.0 4.5 %copy-start.6 = (bf16[512,128]{1,0:T(8,128)(2,1)S(1)}, bf16[512,128]{1,0:T(8,128)(2,1)}, u32[]{:S(2)}) copy-start(bf16[512,128]{1,0:T(8,128)(2,1)} %decode_node_hbm.1) | copy-start | bytes 393220
  0.0 4.5 %copy-start.7 = (bf16[512,128]{1,0:T(8,128)(2,1)S(1)}, bf16[512,128]{1,0:T(8,128)(2,1)}, u32[]{:S(2)}) copy-start(bf16[512,128]{1,0:T(8,128)(2,1)} %decode_grid_hbm.1) | copy-start | bytes 393220
  0.0 4.5 %copy-start.8 = (bf16[84,512]{1,0:T(8,128)(2,1)S(1)}, bf16[84,512]{1,0:T(8,128)(2,1)}, u32[]{:S(2)}) copy-start(bf16[84,512]{1,0:T(8,128)(2,1)} %grid_in.1) | copy-start | bytes 258052
  0.0 4.5 %copy-start.9 = (bf16[84,512]{1,0:T(8,128)(2,1)S(1)}, bf16[84,512]{1,0:T(8,128)(2,1)}, u32[]{:S(2)}) copy-start(bf16[84,512]{1,0:T(8,128)(2,1)} %embed_weight.1) | copy-start | bytes 258052
  0.0 4.5 %copy-start.14 = (s32[1,4,256]{2,1,0:T(4,128)S(1)}, s32[1,4,256]{2,1,0:T(4,128)}, u32[]{:S(2)}) copy-start(s32[1,4,256]{2,1,0:T(4,128)} %cell_lists.1) | copy-start | bytes 12292
  0.1 4.5 %copy-start.15 = (s32[1,1024]{1,0:T(1,128)S(1)}, s32[1,1024]{1,0:T(1,128)}, u32[]{:S(2)}) copy-start(s32[1,1024]{1,0:T(1,128)} %edge_source.1) | copy-start | bytes 12292
  0.1 4.5 %copy-start.16 = (s32[1,1024]{1,0:T(1,128)S(1)}, s32[1,1024]{1,0:T(1,128)}, u32[]{:S(2)}) copy-start(s32[1,1024]{1,0:T(1,128)} %edge_target.1) | copy-start | bytes 12292
  0.1 4.5 %copy-start.18 = (f32[512]{0:T(512)S(1)}, f32[512]{0:T(512)}, u32[]{:S(2)}) copy-start(f32[512]{0:T(512)} %final_gain.1) | copy-start | bytes 6148
  0.1 4.5 %copy-start.19 = (s32[1,4,128]{2,1,0:T(4,128)S(1)}, s32[1,4,128]{2,1,0:T(4,128)}, u32[]{:S(2)}) copy-start(s32[1,4,128]{2,1,0:T(4,128)} %halo_lists.1) | copy-start | bytes 6148
  0.1 4.5 %copy-start.20 = (s32[1,4,128]{2,1,0:T(4,128)S(1)}, s32[1,4,128]{2,1,0:T(4,128)}, u32[]{:S(2)}) copy-start(s32[1,4,128]{2,1,0:T(4,128)} %node_lists.1) | copy-start | bytes 6148
  0.1 4.5 %copy-start.22 = (f32[2,128]{1,0:T(2,128)S(1)}, f32[2,128]{1,0:T(2,128)}, u32[]{:S(2)}) copy-start(f32[2,128]{1,0:T(2,128)} %query_gain.1) | copy-start | bytes 3076
  0.1 4.5 %copy-start.23 = (f32[2,128]{1,0:T(2,128)S(1)}, f32[2,128]{1,0:T(2,128)}, u32[]{:S(2)}) copy-start(f32[2,128]{1,0:T(2,128)} %key_gain.1) | copy-start | bytes 3076
  0.1 4.5 %copy-start.25 = (f32[128]{0:T(128)S(1)}, f32[128]{0:T(128)}, u32[]{:S(2)}) copy-start(f32[128]{0:T(128)} %decode_bias.1) | copy-start | bytes 1540
  2.6 2.0 %copy-start = (bf16[2,512,512]{2,1,0:T(8,128)(2,1)S(1)}, bf16[2,512,512]{2,1,0:T(8,128)(2,1)}, u32[]{:S(2)}) copy-start(bf16[2,512,512]{2,1,0:T(8,128)(2,1)} %hidden_in_hbm.1) | copy-start | bytes 3145732
  2.6 2.0 %copy-start.1 = (bf16[256,512]{1,0:T(8,128)(2,1)S(1)}, bf16[256,512]{1,0:T(8,128)(2,1)}, u32[]{:S(2)}) copy-start(bf16[256,512]{1,0:T(8,128)(2,1)} %mesh_static.1) | copy-start | bytes 786436
  2.6 2.0 %copy-start.2 = (bf16[2,128,512]{2,1,0:T(8,128)(2,1)S(1)}, bf16[2,128,512]{2,1,0:T(8,128)(2,1)}, u32[]{:S(2)}) copy-start(bf16[2,128,512]{2,1,0:T(8,128)(2,1)} %attention_out_hbm.1) | copy-start | bytes 786436
  2.6 2.0 %copy-start.21 = (bf16[4,128]{1,0:T(4,128)(2,1)S(1)}, bf16[4,128]{1,0:T(4,128)(2,1)}, u32[]{:S(2)}) copy-start(bf16[4,128]{1,0:T(4,128)(2,1)} %encode_edge.1) | copy-start | bytes 3076
  2.6 2.0 %copy-start.24 = (f32[128]{0:T(128)S(1)}, f32[128]{0:T(128)}, u32[]{:S(2)}) copy-start(f32[128]{0:T(128)} %encode_bias.1) | copy-start | bytes 1540
  4.2 0.8 %copy-start.10 = (s32[1,32,256]{2,1,0:T(8,128)S(1)}, s32[1,32,256]{2,1,0:T(8,128)}, u32[]{:S(2)}) copy-start(s32[1,32,256]{2,1,0:T(8,128)} %neighbours.1) | copy-start | bytes 98308
  4.3 0.8 %copy-start.11 = (bf16[1,4,1024]{2,1,0:T(4,128)(2,1)S(1)}, bf16[1,4,1024]{2,1,0:T(4,128)(2,1)}, u32[]{:S(2)}) copy-start(bf16[1,4,1024]{2,1,0:T(4,128)(2,1)} %edge_geometry.1) | copy-start | bytes 24580
  4.3 0.7 %copy-start.12 = (s32[3,512]{1,0:T(4,128)S(1)}, s32[3,512]{1,0:T(4,128)}, u32[]{:S(2)}) copy-start(s32[3,512]{1,0:T(4,128)} %cell_nodes.1) | copy-start | bytes 18436
  4.3 0.7 %copy-start.13 = (f32[2,512]{1,0:T(2,128)S(1)}, f32[2,512]{1,0:T(2,128)}, u32[]{:S(2)}) copy-start(f32[2,512]{1,0:T(2,128)} %layer_gain.1) | copy-start | bytes 12292
  4.3 0.7 %copy-start.17 = (f32[512]{0:T(512)S(1)}, f32[512]{0:T(512)}, u32[]{:S(2)}) copy-start(f32[512]{0:T(512)} %embed_bias.1) | copy-start | bytes 6148

commit v2 on v1

--- a/solution.py
+++ b/solution.py
@@ -55,8 +55,34 @@
         )
 
 
-def kernel(
+NEEDED = (
+    (0, 2, 3, 4, 21),
+    (22, 23, 1, 5, 24, 6, 7),
+    (8, 9, 25, 26),
+    (10, 11, 12, 14, 15, 13),
+    (18, 19, 27),
+    (28, 16, 17, 20),
+)
+
+
+def kernel(patches, count, *refs):
+    held, out, local = refs[:count], refs[count], refs[count + 1 : 2 * count + 1]
+    load_sem, rest = refs[2 * count + 1], refs[2 * count + 2 :]
+    loads = [pltpu.make_async_copy(held[i], local[i], load_sem.at[i]) for i in range(count)]
+    for group in NEEDED:
+        for i in group:
+            loads[i].start()
+
+    def need(number):
+        for i in NEEDED[number]:
+            loads[i].wait()
+
+    body(patches, need, *local, out, *rest)
+
+
+def body(
     patches,
+    need,
     grid_in,
     mesh_static,
     embed_weight,
@@ -67,15 +93,15 @@
     encode_bias,
     encode_out,
     layer_gain,
-    attention_in_hbm,
+    attention_in,
     query_gain,
     key_gain,
-    attention_out_hbm,
-    hidden_in_hbm,
-    hidden_out_hbm,
+    attention_out,
+    hidden_in,
+    hidden_out,
     final_gain,
-    decode_node_hbm,
-    decode_grid_hbm,
+    decode_node,
+    decode_grid,
     decode_bias,
     decode_out,
     cell_lists,
@@ -87,12 +113,6 @@
     node_lists,
     cell_nodes,
     out,
-    attention_in,
-    attention_out,
-    hidden_in,
-    hidden_out,
-    decode_node,
-    decode_grid,
     latent_grid,
     cell_hot,
     cell_send,
@@ -117,7 +137,6 @@
     grid_part,
     out_send,
     out_recv,
-    load_sem,
     cell_ssem,
     cell_rsem,
     key_ssem,
@@ -136,22 +155,6 @@
     sibling = m + 1 - 2 * side
     across = (m + 2) % 4
 
-    loads = [
-        pltpu.make_async_copy(src, dst, load_sem.at[i])
-        for i, (src, dst) in enumerate(
-            [
-                (attention_in_hbm, attention_in),
-                (hidden_in_hbm, hidden_in),
-                (hidden_out_hbm, hidden_out),
-                (attention_out_hbm, attention_out),
-                (decode_grid_hbm, decode_grid),
-                (decode_node_hbm, decode_node),
-            ]
-        )
-    ]
-    for load in loads:
-        load.start()
-
     def has_dst(k):
         b = offset_of(k)
         return p + b < patches if b > 0 else p + b >= 0
@@ -188,6 +191,7 @@
                 key_table[layer, k + 1] = jnp.zeros(key_table.shape[2:], BF16)
             node_table[k + 1] = jnp.zeros(node_table.shape[1:], BF16)
 
+    need(0)
     channel_dims = (((0,), (0,)), ((), ()))
     latent_grid[...] = silu(
         lax.dot_general(grid_in[...], embed_weight[...], channel_dims, preferred_element_type=F32)
@@ -248,6 +252,7 @@
     )
     start_all(cell_copies)
 
+    need(1)
     edges = edge_source.shape[1]
     sources = edge_source[0:1, :]
     fill_one_hot(source_hot, 0, sources, 0, source_hot.shape[1])
@@ -268,6 +273,7 @@
     ).astype(BF16)
     node_rows = lax.broadcasted_iota(jnp.int32, (LANES, nodes), 0)
 
+    need(2)
     arrive_all(cell_copies)
     messages = silu(
         pre[...]
@@ -329,8 +335,8 @@
             counts[:, block * LANES : (block + 1) * LANES] = jnp.transpose(total)
 
     def prepare_decode():
-        loads[4].wait()
-        loads[5].wait()
+        need(4)
+        need(5)
         grid_part[...] = dot(latent_grid[...], decode_grid[...]) + decode_bias[...][None, :]
         for k in range(near):
             fill_one_hot(list_hot, k * cap_node, node_lists[0, k : k + 1, :], 0, nodes)
@@ -345,9 +351,11 @@
     node_copies_key = []
     for layer in range(LAYERS):
         if layer == 0:
-            loads[0].wait()
+            need(3)
         rows = normed[layer]
-        projections = dot(rows, attention_in[layer])
+        projections = dot(
+            rows, jnp.concatenate([attention_in[layer, kind] for kind in range(3)], axis=1)
+        )
         queries = rms_scale(projections[:, :width], query_gain[layer : layer + 1, :]).astype(BF16)
         keys = rms_scale(projections[:, width : 2 * width], key_gain[layer : layer + 1, :]).astype(
             BF16
@@ -365,9 +373,6 @@
         )
         start_all(copies)
         node_copies_key.append(copies)
-        if layer == 0:
-            for load in loads[1:4]:
-                load.wait()
         hidden = silu(dot(rows, hidden_in[layer])).astype(BF16)
         part = dot(hidden, hidden_out[layer])
         last = (((1,), (1,)), ((), ()))
@@ -413,11 +418,11 @@
     activity = silu(chosen[:cells] + grid_part[...])
     for j in range(1, 3):
         activity = activity + silu(chosen[j * cells : (j + 1) * cells] + grid_part[...])
-    channels = decode_out.shape[1]
+    channels = decode_out.shape[0]
     term = lax.dot_general(
         decode_out[...],
         activity.astype(BF16),
-        (((0,), (1,)), ((), ())),
+        (((1,), (1,)), ((), ())),
         preferred_element_type=F32,
     )
     padding = out_send.shape[1] - channels
@@ -450,10 +455,9 @@
     operands = list(operands)
     (grid_in, mesh_static, embed_weight) = operands[:3]
     attention_in = operands[10]
-    layers, depth, kinds, width = attention_in.shape
-    operands[10] = attention_in.reshape(layers, depth, kinds * width)
-    attention_out, hidden_in, hidden_out = operands[13:16]
-    decode_node, decode_grid = operands[17:19]
+    layers, _, _, width = attention_in.shape
+    operands[10] = jnp.transpose(attention_in, (0, 2, 1, 3))
+    operands[20] = operands[20].T
     cell_lists, edge_source = operands[21:23]
     halo_lists, neighbours, node_lists, cell_nodes = operands[25:29]
     channels, cells = grid_in.shape
@@ -466,13 +470,9 @@
     padded = -(-channels // 16) * 16
     sums = layers + 1
     vmem, dma = pltpu.VMEM, pltpu.SemaphoreType.DMA
-    scratch = [
-        vmem(operands[10].shape, BF16),
-        vmem(attention_out.shape, BF16),
-        vmem(hidden_in.shape, BF16),
-        vmem(hidden_out.shape, BF16),
-        vmem(decode_node.shape, BF16),
-        vmem(decode_grid.shape, BF16),
+    scratch = [vmem(operand.shape, operand.dtype) for operand in operands]
+    scratch += [
+        dma((len(operands),)),
         vmem((cells, features), BF16),
         vmem((near * cap_cell, cells), BF16),
         vmem((near, cap_cell, width), BF16),
@@ -497,7 +497,6 @@
         vmem((cells, width), F32),
         vmem((2, padded, cells), BF16),
         vmem((2, padded, cells), BF16),
-        dma((6,)),
         dma((near,)),
         dma((near,)),
         dma((layers, near)),
@@ -509,18 +508,14 @@
         dma((2,)),
         dma((2,)),
     ]
-    in_hbm = (10, 13, 14, 15, 17, 18)
     return pl.pallas_call(
-        functools.partial(kernel, patches),
+        functools.partial(kernel, patches, len(operands)),
         out_shape=jax.ShapeDtypeStruct((channels, cells), BF16),
-        in_specs=[
-            pl.BlockSpec(memory_space=pl.ANY if i in in_hbm else pltpu.VMEM)
-            for i in range(len(operands))
-        ],
+        in_specs=[pl.BlockSpec(memory_space=pltpu.HBM)] * len(operands),
         out_specs=pl.BlockSpec(memory_space=pltpu.VMEM),
         scratch_shapes=scratch,
         compiler_params=pltpu.CompilerParams(
-            collective_id=0, has_side_effects=True, vmem_limit_bytes=50 * 1024 * 1024
+            collective_id=0, has_side_effects=True, vmem_limit_bytes=64 * 1024 * 1024
         ),
         name="denoise",
     )(*operands)

time: 64 us -> 60.1 us (0.939)
  local copies, waits for them, and re-layouts: 5.32 us -> 1.53 us
    unnamed x57 -> x1, local copies, waits for them, and re-layouts: 3.72 us -> 1.53 us
    reshape x1 -> x0, local copies, waits for them, and re-layouts: 1.61 us -> none  [shards(): operands[10] = attention_in.reshape(layers, depth, kinds * width)]
where the time goes in v2:
time: 60.1 us; the launch traced here: 59.9 us
  Pallas kernels  58.4 us (97%)
  local copies, waits for them, and re-layouts  1.53 us (3%)
    pallas_call x1, Pallas kernels, shards(): pl.pallas_call(functools.partial(kernel, patches, len(operands)), out_sha...  58.4 us
    unnamed x1, local copies, waits for them, and re-layouts  1.53 us

profile of v2, /device:TPU:0, one launch (start us, length us, event | category | flops | bytes accessed | tf_op | source)
XLA Modules:
  0.0 59.9 jit_solution(16291372535123556459)
XLA Ops:
  0.0 58.4 %denoise.1 = bf16[84,512]{1,0:T(8,128)(2,1)} custom-call(bf16[84,512]{1,0:T(8,128)(2,1)} %refs_0_.1, bf16[256,512]{1,0:T(8,128)(2,1)} %refs_1_.1, bf16[84,512]{1,0:T(8,128)(2,1)} %refs_2_.1, f32[512]{0:T(512)} %refs_3_.1, bf16[512,128]{1,0:T(8,128)(2,1)} %refs_4_.1, bf16[512,128]{1,0:T(8,128)(2,1)} %refs_5_.1, bf16[4,128]{1,0:T(4,128)(2,1)} %refs_6_.1, ...), custom_call_target="tpu_custom_call" | custom-call | tf_op jit(solution)/shard_map/denoise/pallas_call | solution.py:511
  58.4 1.5 %copy.31 = bf16[84,512]{1,0:T(8,128)(2,1)} copy(bf16[84,512]{1,0:T(8,128)(2,1)} %denoise.1) | data formatting | bytes 172032
